TPU v7x, 32 devices: a whole 2x2x4 slice. The times are simulated.
32 devices in a mesh: rep: 4 (over y, core), shard: 8 (over z, x).
Axes of the slice: x: 2, y: 2, z: 4, core: 2. Of those that a mesh axis runs over, the one named last changes fastest.
Arguments:
- hidden_in: bfloat16 [32768, 768], P(('rep', 'shard')), may hold values from -6 to 6
- seq_lengths: int32 [32, 8], P(('rep', 'shard')), may hold values from 0 to 1024, as said below
- norm1_scale: bfloat16 [768], P('shard'), may hold values from 0.099609375 to 1.8984375
- qkv_weight: bfloat16 [768, 2304], P('shard'), may hold values from -0.21875 to 0.21875
- out_weight: bfloat16 [768, 768], P('shard'), may hold values from -1.75 to 1.75
- norm2_scale: bfloat16 [768], P('shard'), may hold values from 0.099609375 to 1.8984375
- in_weight: bfloat16 [768, 2304], P('shard'), may hold values from -0.21875 to 0.21875
- mlp_out_weight: bfloat16 [1152, 768], P('shard'), may hold values from -0.1875 to 0.1875
- cotangent: bfloat16 [32768, 768], P(('rep', 'shard')), may hold values from -6 to 6
Outputs:
- output: bfloat16 [32768, 768], P(('rep', 'shard'))
- input_grad: bfloat16 [32768, 768], P(('rep', 'shard'))
- norm1_grad: float32 [768], P('shard')
- qkv_grad: float32 [768, 2304], P('shard')
- out_grad: float32 [768, 768], P('shard')
- norm2_grad: float32 [768], P('shard')
- in_grad: float32 [768, 2304], P('shard')
- mlp_out_grad: float32 [1152, 768], P('shard')
Inputs may be any that keep to these rules, and one draw needn't show every extreme that they name: `seq_lengths`: each row lists one device's sequence lengths in order, then zeros; a nonzero length is at least 64; a row sums to at most 1024 and at least 512; some row holds a single sequence of 1024 tokens.
All inputs are finite; a program needn't handle non-finite values.
Results may differ from a plain program's by a relative error of at most 0.015.
Values may be sent and summed in bfloat16 or wider, within the bound.
A program may use at most 256 MiB of HBM per device.

v0:
```python
import jax
import jax.numpy as jnp
from jax import lax
from jax.sharding import PartitionSpec as P

HEADS = 12


rope_base = 160000.0
norm_eps = 1e-05
masked_score = -1000000000.0


def layer_norm(values, gain_vec):
    centered = values - jnp.mean(values, axis=-1, keepdims=True)
    spread = jnp.mean(centered * centered, axis=-1, keepdims=True)
    return centered * lax.rsqrt(spread + norm_eps) * gain_vec


def rotary_tables(lengths, token_rows, head_width):
    seq_ends = jnp.cumsum(lengths)
    row_ids = jnp.arange(token_rows, dtype=jnp.int32)
    passed = row_ids[:, None] >= seq_ends[None, :]
    segment = jnp.sum(passed.astype(jnp.int32), axis=1)
    starts = jnp.sum(jnp.where(passed, lengths[None, :], 0), axis=1)
    position = (row_ids - starts).astype(jnp.float32)
    half_width = head_width // 2
    frequency = rope_base ** (-(jnp.arange(half_width, dtype=jnp.float32) * 2.0 / head_width))
    angles = position[:, None] * frequency[None, :]
    valid_rows = (row_ids < seq_ends[-1]).astype(jnp.float32)
    return (jnp.cos(angles), jnp.sin(angles), segment, valid_rows)


def rope(tensor, cosine, sine_table):
    half_width = tensor.shape[-1] // 2
    first = tensor[..., :half_width]
    second = tensor[..., half_width:]
    cos_b = cosine[:, None, :]
    sin_b = sine_table[:, None, :]
    return jnp.concatenate(
        [first * cos_b - second * sin_b, second * cos_b + first * sin_b], axis=-1
    )


def geglu(gate_up):
    hidden_units = gate_up.shape[-1] // 2
    return jax.nn.gelu(gate_up[:, :hidden_units], approximate=False) * gate_up[:, hidden_units:]


def per_device(
    hidden_in,
    seq_lengths,
    norm1_scale,
    qkv_weight,
    out_weight,
    norm2_scale,
    in_weight,
    mlp_out_weight,
    cotangent,
):
    token_rows, model_width = hidden_in.shape
    head_count = HEADS
    head_width = model_width // head_count
    block_rows = min(512, token_rows)
    block_count = token_rows // block_rows
    score_scale = head_width ** (-0.5)
    cosine, sine_table, segment, valid_rows = rotary_tables(seq_lengths[0], token_rows, head_width)
    gathered = (
        lax.all_gather(norm1_scale, "shard", axis=0, tiled=True),
        lax.all_gather(qkv_weight, "shard", axis=0, tiled=True),
        lax.all_gather(out_weight, "shard", axis=0, tiled=True),
        lax.all_gather(norm2_scale, "shard", axis=0, tiled=True),
        lax.all_gather(in_weight, "shard", axis=0, tiled=True),
        lax.all_gather(mlp_out_weight, "shard", axis=0, tiled=True),
    )
    inputs_f32 = hidden_in.astype(jnp.float32)
    normed_one = layer_norm(inputs_f32, gathered[0].astype(jnp.float32)).astype(jnp.bfloat16)
    projected = jnp.dot(normed_one, gathered[1], preferred_element_type=jnp.float32).reshape(
        token_rows, 3, head_count, head_width
    )
    queries = rope(projected[:, 0], cosine, sine_table).astype(jnp.bfloat16)
    keys_rot = rope(projected[:, 1], cosine, sine_table).astype(jnp.bfloat16)
    values_low = projected[:, 2].astype(jnp.bfloat16)
    query_blocks = queries.reshape(block_count, block_rows, head_count, head_width)
    seg_blocks = segment.reshape(block_count, block_rows)

    def block_scores(query_block, seg_block):
        scores = (
            jnp.einsum("qhd,khd->hqk", query_block, keys_rot, preferred_element_type=jnp.float32)
            * score_scale
        )
        same_seq = seg_block[:, None] == segment[None, :]
        return jnp.where(same_seq[None], scores, masked_score)

    def forward_block(pieces):
        query_block, seg_block = pieces
        scores = block_scores(query_block, seg_block)
        row_max = jnp.max(scores, axis=-1, keepdims=True)
        log_total = row_max + jnp.log(jnp.sum(jnp.exp(scores - row_max), axis=-1, keepdims=True))
        prob_low = jnp.exp(scores - log_total).astype(jnp.bfloat16)
        attended = jnp.einsum(
            "hqk,khd->qhd", prob_low, values_low, preferred_element_type=jnp.float32
        )
        return (attended, log_total)

    attended, log_totals = lax.map(forward_block, (query_blocks, seg_blocks))
    attn_low = attended.reshape(token_rows, model_width).astype(jnp.bfloat16)
    resid_one = inputs_f32 + jnp.dot(attn_low, gathered[2], preferred_element_type=jnp.float32)
    normed_two = layer_norm(resid_one, gathered[3].astype(jnp.float32)).astype(jnp.bfloat16)
    gate_up = jnp.dot(normed_two, gathered[4], preferred_element_type=jnp.float32)
    mixed_low = geglu(gate_up).astype(jnp.bfloat16)
    result = valid_rows[:, None] * (
        resid_one + jnp.dot(mixed_low, gathered[5], preferred_element_type=jnp.float32)
    )
    output = result.astype(jnp.bfloat16)
    again = (
        lax.all_gather(norm1_scale, "shard", axis=0, tiled=True),
        lax.all_gather(qkv_weight, "shard", axis=0, tiled=True),
        lax.all_gather(out_weight, "shard", axis=0, tiled=True),
        lax.all_gather(norm2_scale, "shard", axis=0, tiled=True),
        lax.all_gather(in_weight, "shard", axis=0, tiled=True),
        lax.all_gather(mlp_out_weight, "shard", axis=0, tiled=True),
    )
    cot_rows = cotangent.astype(jnp.float32) * valid_rows[:, None]
    mlp_cot = cot_rows.astype(jnp.bfloat16)
    grad_mlp_out = jnp.einsum("nf,nd->fd", mixed_low, mlp_cot, preferred_element_type=jnp.float32)
    grad_mixed = jnp.einsum("nd,fd->nf", mlp_cot, again[5], preferred_element_type=jnp.float32)
    _, geglu_back = jax.vjp(geglu, gate_up)
    grad_gate_up = geglu_back(grad_mixed)[0].astype(jnp.bfloat16)
    grad_in_w = jnp.einsum(
        "nd,nf->df", normed_two, grad_gate_up, preferred_element_type=jnp.float32
    )
    grad_normed_two = jnp.einsum(
        "nf,df->nd", grad_gate_up, again[4], preferred_element_type=jnp.float32
    )
    _, norm_two_back = jax.vjp(layer_norm, resid_one, again[3].astype(jnp.float32))
    grad_resid_ln, grad_gain_two = norm_two_back(grad_normed_two)
    grad_resid = cot_rows + grad_resid_ln
    attn_cot = grad_resid.astype(jnp.bfloat16)
    grad_out_w = jnp.einsum("nd,ne->de", attn_low, attn_cot, preferred_element_type=jnp.float32)
    grad_attn = jnp.einsum(
        "ne,de->nd", attn_cot, again[2], preferred_element_type=jnp.float32
    ).astype(jnp.bfloat16)
    grad_attn = grad_attn.reshape(block_count, block_rows, head_count, head_width)

    def backward_block(running, pieces):
        key_acc, value_acc = running
        query_block, seg_block, grad_block, log_total = pieces
        scores = block_scores(query_block, seg_block)
        prob_f32 = jnp.exp(scores - log_total)
        prob_low = prob_f32.astype(jnp.bfloat16)
        grad_prob = jnp.einsum(
            "qhd,khd->hqk", grad_block, values_low, preferred_element_type=jnp.float32
        )
        value_acc = value_acc + jnp.einsum(
            "hqk,qhd->khd", prob_low, grad_block, preferred_element_type=jnp.float32
        )
        row_delta = jnp.sum(prob_f32 * grad_prob, axis=-1, keepdims=True)
        grad_scores = (prob_f32 * (grad_prob - row_delta)).astype(jnp.bfloat16)
        grad_query = (
            jnp.einsum("hqk,khd->qhd", grad_scores, keys_rot, preferred_element_type=jnp.float32)
            * score_scale
        )
        key_acc = (
            key_acc
            + jnp.einsum(
                "hqk,qhd->khd", grad_scores, query_block, preferred_element_type=jnp.float32
            )
            * score_scale
        )
        return ((key_acc, value_acc), grad_query)

    empty = jnp.zeros((token_rows, head_count, head_width), jnp.float32)
    (grad_keys, grad_values), grad_queries = lax.scan(
        backward_block, (empty, empty), (query_blocks, seg_blocks, grad_attn, log_totals)
    )
    grad_queries = grad_queries.reshape(token_rows, head_count, head_width)
    _, rope_back = jax.vjp(lambda tensor: rope(tensor, cosine, sine_table), projected[:, 0])
    grad_projected = jnp.stack(
        [rope_back(grad_queries)[0], rope_back(grad_keys)[0], grad_values], axis=1
    )
    grad_projected = grad_projected.reshape(token_rows, 3 * model_width).astype(jnp.bfloat16)
    grad_qkv_w = jnp.einsum(
        "nd,ne->de", normed_one, grad_projected, preferred_element_type=jnp.float32
    )
    grad_normed_one = jnp.einsum(
        "ne,de->nd", grad_projected, again[1], preferred_element_type=jnp.float32
    )
    _, norm_one_back = jax.vjp(layer_norm, inputs_f32, again[0].astype(jnp.float32))
    grad_input_ln, grad_gain_one = norm_one_back(grad_normed_one)
    input_grad = (grad_resid + grad_input_ln).astype(jnp.bfloat16)
    owned = (
        lax.psum_scatter(grad_gain_one, "shard", scatter_dimension=0, tiled=True),
        lax.psum_scatter(grad_qkv_w, "shard", scatter_dimension=0, tiled=True),
        lax.psum_scatter(grad_out_w, "shard", scatter_dimension=0, tiled=True),
        lax.psum_scatter(grad_gain_two, "shard", scatter_dimension=0, tiled=True),
        lax.psum_scatter(grad_in_w, "shard", scatter_dimension=0, tiled=True),
        lax.psum_scatter(grad_mlp_out, "shard", scatter_dimension=0, tiled=True),
    )
    owned = lax.psum((owned[0], owned[1], owned[2], owned[3], owned[4], owned[5]), "rep")
    return (output, input_grad, owned[0], owned[1], owned[2], owned[3], owned[4], owned[5])


def solution(mesh):
    return jax.shard_map(
        per_device,
        mesh=mesh,
        in_specs=(
            P(("rep", "shard"), None),
            P(("rep", "shard"), None),
            P("shard"),
            P("shard", None),
            P("shard", None),
            P("shard"),
            P("shard", None),
            P("shard", None),
            P(("rep", "shard"), None),
        ),
        out_specs=(
            P(("rep", "shard"), None),
            P(("rep", "shard"), None),
            P("shard"),
            P("shard", None),
            P("shard", None),
            P("shard"),
            P("shard", None),
            P("shard", None),
        ),
        check_vma=False,
    )
```

profile of v0, /device:TPU:11, one launch (start us, length us, event | category | flops | bytes accessed | tf_op | source)
XLA Modules:
  0.0 766.7 jit_solution(14895937830536304876)
XLA Ops:
  15.1 12.3 %all-reduce.13 = (bf16[768]{0:T(1024)(128)(2,1)S(1)}, bf16[768]{0:T(1024)(128)(2,1)S(1)}) all-reduce(bf16[768]{0:T(1024)(128)(2,1)S(1)} %dynamic-update-slice, bf16[768]{0:T(1024)(128)(2,1)S(1)} %dynamic-update-slice.1), channel_id=1, replica_groups=mesh['rep'=4,'shard'=8] {'shard'}, use_global_device_ids=true, to_apply=%add.6 | all-reduce | flops 1536 | bytes 6144
  30.1 1.8 copy.52
  33.3 1.7 copy.58
  35.5 38.8 %all-gather.5.cloned.1.call-done = bf16[768,2304]{1,0:T(8,128)(2,1)} async-done(((bf16[96,2304]{1,0:T(8,128)(2,1)}), bf16[768,2304]{1,0:T(8,128)(2,1)}) %all-gather.5.cloned.1.call-update) | async-done | bytes 3538960 | tf_op jit(solution)/shard_map/all_gather | solution.py:70
  74.3 6.3 fusion.63
  80.7 1.4 fusion.52
  86.4 75.3 %while.27 = (s32[]{:T(128)}, bf16[2,512,12,64]{1,3,2,0:T(8,128)(2,1)}, f32[2,12,512,1]{2,1,3,0:T(8,128)S(1)}, s32[2,512]{1,0:T(2,128)S(1)}, s32[1024]{0:T(1024)S...) while((s32[]{:T(128)}, ...), condition=%wide.region_8.9_spmd, body=%wide.region_5.8_spmd.sunk | while | flops 1680336896 | bytes 95930536 | solution.py:106
  87.0 12.0 %fusion.114 = (f32[12,512]{1,0:T(8,128)S(1)}, f32[12,512,1024]{2,1,0:T(8,128)}) fusion(pred[512,1024]{1,0:T(8,128)(4,1)S(1)} %broadcast_compare_fusion.4, bf16[1024,12,64]{0,2,1:T(8,128)(2,1)S(1)} %get-tuple-element.471, bf16[2,512,12,64]{1,3,2,0:T(8,128)(2,1)} %get-tuple-element.470, s32[]{:T(128)S(6)} %copy.100), kind=kOutput, calls=%fused_computation.3.clone.1 | convolution fusion | flops 824174592 | bytes 28073988 | tf_op jit(solution)/shard_map/while/body/eval_jaxpr/qhd,khd->hqk/dot_general | solution.py:89
  99.0 12.0 %exponential_reduce_fusion.2 = f32[12,512]{1,0:T(8,128)S(1)} fusion(f32[12,512,1024]{2,1,0:T(8,128)} %get-tuple-element.430, f32[12,512]{1,0:T(8,128)S(1)} %get-tuple-element.431, pred[512,1024]{1,0:T(8,128)(4,1)S(1)} %broadcast_compare_fusion.4), kind=kLoop, calls=%fused_computation.1.clone.1 | loop fusion | flops 25159680 | bytes 25739264 | tf_op jit(solution)/shard_map/while/body/eval_jaxpr/reduce_sum | solution.py:99
  111.0 11.6 %bitcast_dynamic-update-slice_fusion.7 = bf16[2,512,12,64]{1,3,2,0:T(8,128)(2,1)S(1)} fusion(bf16[2,512,12,64]{1,3,2,0:T(8,128)(2,1)S(1)} %copy-done.14, s32[]{:T(128)S(6)} %copy.100, bf16[1024,12,64]{0,2,1:T(8,128)(2,1)} %get-tuple-element.472, f32[12,512,1024]{2,1,0:T(8,128)} %get-tuple-element.430, f32[12,512]{1,0:T(8,128)S(1)} %get-tuple-element.432, ...), kind=kOutput, calls=%fused_computation.6.clone.1 | convolution fusion | flops 830472192 | bytes 28868612 | tf_op jit(solution)/shard_map/while/body/eval_jaxpr/hqk,khd->qhd/dot_general | solution.py:101
  124.2 12.0 %fusion.114 = (f32[12,512]{1,0:T(8,128)S(1)}, f32[12,512,1024]{2,1,0:T(8,128)}) fusion(pred[512,1024]{1,0:T(8,128)(4,1)S(1)} %broadcast_compare_fusion.4, bf16[1024,12,64]{0,2,1:T(8,128)(2,1)S(1)} %get-tuple-element.471, bf16[2,512,12,64]{1,3,2,0:T(8,128)(2,1)} %get-tuple-element.470, s32[]{:T(128)S(6)} %copy.100), kind=kOutput, calls=%fused_computation.3.clone.1 | convolution fusion | flops 824174592 | bytes 28073988 | tf_op jit(solution)/shard_map/while/body/eval_jaxpr/qhd,khd->hqk/dot_general | solution.py:89
  136.2 11.9 %exponential_reduce_fusion.2 = f32[12,512]{1,0:T(8,128)S(1)} fusion(f32[12,512,1024]{2,1,0:T(8,128)} %get-tuple-element.430, f32[12,512]{1,0:T(8,128)S(1)} %get-tuple-element.431, pred[512,1024]{1,0:T(8,128)(4,1)S(1)} %broadcast_compare_fusion.4), kind=kLoop, calls=%fused_computation.1.clone.1 | loop fusion | flops 25159680 | bytes 25739264 | tf_op jit(solution)/shard_map/while/body/eval_jaxpr/reduce_sum | solution.py:99
  148.2 12.1 %bitcast_dynamic-update-slice_fusion.7 = bf16[2,512,12,64]{1,3,2,0:T(8,128)(2,1)S(1)} fusion(bf16[2,512,12,64]{1,3,2,0:T(8,128)(2,1)S(1)} %copy-done.14, s32[]{:T(128)S(6)} %copy.100, bf16[1024,12,64]{0,2,1:T(8,128)(2,1)} %get-tuple-element.472, f32[12,512,1024]{2,1,0:T(8,128)} %get-tuple-element.430, f32[12,512]{1,0:T(8,128)S(1)} %get-tuple-element.432, ...), kind=kOutput, calls=%fused_computation.6.clone.1 | convolution fusion | flops 830472192 | bytes 28868612 | tf_op jit(solution)/shard_map/while/body/eval_jaxpr/hqk,khd->qhd/dot_general | solution.py:101
  161.7 3.1 copy.56
  164.8 1.6 copy.86
  166.4 3.3 fusion.74
  171.3 11.0 %all-gather.9.cloned.1.call-done = bf16[768,2304]{1,0:T(8,128)(2,1)} async-done(((bf16[96,2304]{1,0:T(8,128)(2,1)}), bf16[768,2304]{1,0:T(8,128)(2,1)}) %all-gather.9.cloned.1.call-update) | async-done | bytes 3538960 | tf_op jit(solution)/shard_map/all_gather | solution.py:73
  182.3 10.6 %fusion.70 = f32[1024,2304]{1,0:T(8,128)} fusion(bf16[768,2304]{1,0:T(8,128)(2,1)} %all-gather.9.cloned.1.call-done, f32[1024,768]{0,1:T(8,128)} %copy-done.8, f32[768]{0:T(1024)S(1)} %copy-done.36, f32[1024]{0:T(1024)S(1)} %fusion.67, f32[1024]{0:T(1024)S(1)} %broadcast_multiply_fusion), kind=kOutput, calls=%fused_computation.141 | convolution fusion | flops 3627024384 | bytes 16133120 | tf_op jit(solution)/shard_map/dot_general | solution.py:110
  192.9 37.3 %all-gather.11.cloned.1.call-done = bf16[1152,768]{1,0:T(8,128)(2,1)} async-done(((bf16[144,768]{1,0:T(8,128)(2,1)}), bf16[1152,768]{1,0:T(8,128)(2,1)}) %all-gather.11.cloned.1.call-update) | async-done | bytes 1769488 | tf_op jit(solution)/shard_map/all_gather | solution.py:74
  230.2 27.1 %fusion.53 = (f32[1024,1152]{1,0:T(8,128)}, f32[1024,1152]{1,0:T(8,128)S(1)}, f32[1024,1152]{1,0:T(8,128)S(1)}) fusion(f32[1024,2304]{1,0:T(8,128)} %fusion.70, bf16[1152,768]{1,0:T(8,128)(2,1)} %all-gather.11.cloned.1.call-done, bf16[1024,768]{0,1:T(8,128)(2,1)S(1)} %copy-done.6, f32[1024]{0:T(1024)S(1)} %copy-done.28), kind=kOutput, calls=%fused_computation.110 | convolution fusion | flops 1890975744 | bytes 22220800 | tf_op jit(solution)/shard_map/nd,fd->nf/dot_general | solution.py:127
  257.3 3.5 multiply_add_fusion
  260.8 9.6 %multiply_reduce_fusion.1 = (f32[768]{0:T(1024)}, f32[1024]{0:T(1024)S(1)}, f32[1024,768]{0,1:T(8,128)S(1)}) fusion(f32[1024,768]{0,1:T(8,128)S(1)} %copy-done.9, f32[1024]{0:T(1024)S(1)} %fusion.67, f32[1024]{0:T(1024)S(1)} %broadcast_multiply_fusion, f32[768]{0:T(1024)S(1)} %copy-done.36, bf16[768,2304]{1,0:T(8,128)(2,1)} %all-gather.9.cloned.1.call-done, ...), kind=kOutput, calls=%fused_computation.84 | convolution fusion | flops 3634100480 | bytes 19286016 | tf_op jit(solution)/shard_map/nf,df->nd/dot_general | solution.py:133
  274.2 3.0 fusion.75
  277.3 5.5 fusion.54
  284.2 4.0 convolution_convert_fusion
  288.2 1.7 copy.59
  289.9 2.4 reshape.258
  292.3 2.9 copy.60
  295.2 11.6 %fusion.58 = f32[768,2304]{1,0:T(8,128)} fusion(f32[1024,1152]{1,0:T(8,128)} %copy-done.11, f32[1024,1152]{1,0:T(8,128)} %get-tuple-element.285, f32[1024,768]{0,1:T(8,128)} %copy-done.8, f32[768]{0:T(1024)S(1)} %copy-done.36, f32[1024]{0:T(1024)S(1)} %fusion.67, f32[1024]{0:T(1024)S(1)} %broadcast_multiply_fusion), kind=kOutput, calls=%fused_computation.115 | convolution fusion | flops 3631742976 | bytes 19672064 | tf_op jit(solution)/shard_map/nd,nf->df/dot_general | solution.py:130
  306.9 233.0 %while.28 = (s32[]{:T(128)}, f32[1024,12,64]{0,2,1:T(8,128)}, f32[1024,12,64]{0,2,1:T(8,128)}, f32[2,512,12,64]{1,0,3,2:T(2,128)}, bf16[2,512,12,64]{1,3,2,0:T(8...) while((s32[]{:T(128)}, f32[1024,12,64]{0,2,1:T(8,128)}, ...), condition=%wide.region_15.16_spmd.clone, body=%wide.region_13.15_spmd.clone.sunk | while | flops 4125747200 | bytes 231925968 | solution.py:174
  307.7 11.6 %fusion.124 = f32[12,512,1024]{2,1,0:T(8,128)} fusion(bf16[1024,12,64]{0,2,1:T(8,128)(2,1)S(1)} %get-tuple-element.507, bf16[2,512,12,64]{1,3,2,0:T(8,128)(2,1)} %get-tuple-element.504, s32[]{:T(128)S(6)} %copy.110), kind=kOutput, calls=%fused_computation.31.clone.1 | convolution fusion | flops 805306368 | bytes 27525124 | tf_op jit(solution)/shard_map/while/body/eval_jaxpr/qhd,khd->hqk/dot_general | solution.py:89
  319.3 13.5 %bitcast_add_fusion.5 = f32[1024,12,64]{0,2,1:T(8,128)} fusion(f32[1024,12,64]{0,2,1:T(8,128)} %get-tuple-element.489, f32[12,512,1024]{2,1,0:T(8,128)} %fusion.124, f32[12,512]{1,0:T(8,128)S(1)} %dynamic-slice_bitcast_fusion.2, pred[512,1024]{1,0:T(8,128)(4,1)S(1)} %broadcast_compare_fusion.5, pred[]{:T(512)S(6)} %compare.9, ...), kind=kOutput, calls=%fused_computation.23.clone.1 | convolution fusion | flops 832045056 | bytes 32800772 | tf_op jit(solution)/shard_map/while/body/eval_jaxpr/hqk,qhd->khd/dot_general | solution.py:155
  332.8 18.1 %multiply_reduce_fusion.5 = (f32[12,512]{1,0:T(8,128)S(1)}, f32[12,512,1024]{2,1,0:T(8,128)}) fusion(f32[12,512,1024]{2,1,0:T(8,128)} %fusion.124, f32[12,512]{1,0:T(8,128)S(1)} %dynamic-slice_bitcast_fusion.2, pred[512,1024]{1,0:T(8,128)(4,1)S(1)} %broadcast_compare_fusion.5, bf16[1024,12,64]{0,2,1:T(8,128)(2,1)} %get-tuple-element.510, ...), kind=kOutput, calls=%fused_computation.18.clone.1 | convolution fusion | flops 836757504 | bytes 53264388 | tf_op jit(solution)/shard_map/while/body/eval_jaxpr/qhd,khd->hqk/dot_general | solution.py:152
  351.0 21.8 %multiply_convert_fusion.7 = bf16[12,512,1024]{2,1,0:T(8,128)(2,1)} fusion(f32[12,512,1024]{2,1,0:T(8,128)} %get-tuple-element.445, f32[12,512,1024]{2,1,0:T(8,128)} %fusion.124, f32[12,512]{1,0:T(8,128)S(1)} %get-tuple-element.446, f32[12,512]{1,0:T(8,128)S(1)} %dynamic-slice_bitcast_fusion.2, pred[512,1024]{1,0:T(8,128)(4,1)S(1)} %broadcast_compare_fusion.5), kind=kLoop, calls=%fused_computation.17.clone.1 | loop fusion | flops 37748736 | bytes 63488000 | tf_op jit(solution)/shard_map/while/body/eval_jaxpr/convert_element_type | solution.py:159
  372.8 9.8 %multiply_bitcast_fusion.2 = f32[1,512,12,64]{1,3,2,0:T(8,128)} fusion(bf16[12,512,1024]{2,1,0:T(8,128)(2,1)} %multiply_convert_fusion.7, bf16[1024,12,64]{0,2,1:T(8,128)(2,1)S(1)} %get-tuple-element.507), kind=kOutput, calls=%fused_computation.25.clone.1 | convolution fusion | flops 805699584 | bytes 15728640 | tf_op jit(solution)/shard_map/while/body/eval_jaxpr/hqk,khd->qhd/dot_general | solution.py:161
  382.6 9.1 %bitcast_add_fusion.4 = f32[1024,12,64]{0,2,1:T(8,128)} fusion(f32[1024,12,64]{0,2,1:T(8,128)} %get-tuple-element.488, bf16[12,512,1024]{2,1,0:T(8,128)(2,1)} %multiply_convert_fusion.7, pred[]{:T(512)S(6)} %compare.9, bf16[2,512,12,64]{1,3,2,0:T(8,128)(2,1)} %get-tuple-element.504, s32[]{:T(128)S(6)} %copy.110), kind=kOutput, calls=%fused_computation.24.clone.1 | convolution fusion | flops 807665664 | bytes 19660804 | tf_op jit(solution)/shard_map/while/body/eval_jaxpr/hqk,qhd->khd/dot_general | solution.py:166
  391.7 1.6 copy.90
  393.3 28.7 %dynamic_update_slice.19 = f32[2,512,12,64]{1,0,3,2:T(2,128)} dynamic-update-slice(f32[2,512,12,64]{1,0,3,2:T(2,128)} %get-tuple-element.490, f32[1,512,12,64]{1,0,3,2:T(1,128)S(1)} %copy.90, s32[]{:T(128)S(6)} %copy.110, s32[]{:T(128)} %constant.33.clone.1..sunk, s32[]{:T(128)} %constant.33.clone.1..sunk, s32[]{:T(128)} %constant.33.clone.1..sunk) | dynamic-update-slice | bytes 3145732 | tf_op jit(solution)/shard_map/while/body/jit(dynamic_update_index_in_dim)/dynamic_update_slice | solution.py:106
  422.5 11.5 %fusion.124 = f32[12,512,1024]{2,1,0:T(8,128)} fusion(bf16[1024,12,64]{0,2,1:T(8,128)(2,1)S(1)} %get-tuple-element.507, bf16[2,512,12,64]{1,3,2,0:T(8,128)(2,1)} %get-tuple-element.504, s32[]{:T(128)S(6)} %copy.110), kind=kOutput, calls=%fused_computation.31.clone.1 | convolution fusion | flops 805306368 | bytes 27525124 | tf_op jit(solution)/shard_map/while/body/eval_jaxpr/qhd,khd->hqk/dot_general | solution.py:89
  433.9 15.0 %bitcast_add_fusion.5 = f32[1024,12,64]{0,2,1:T(8,128)} fusion(f32[1024,12,64]{0,2,1:T(8,128)} %get-tuple-element.489, f32[12,512,1024]{2,1,0:T(8,128)} %fusion.124, f32[12,512]{1,0:T(8,128)S(1)} %dynamic-slice_bitcast_fusion.2, pred[512,1024]{1,0:T(8,128)(4,1)S(1)} %broadcast_compare_fusion.5, pred[]{:T(512)S(6)} %compare.9, ...), kind=kOutput, calls=%fused_computation.23.clone.1 | convolution fusion | flops 832045056 | bytes 32800772 | tf_op jit(solution)/shard_map/while/body/eval_jaxpr/hqk,qhd->khd/dot_general | solution.py:155
  449.0 18.2 %multiply_reduce_fusion.5 = (f32[12,512]{1,0:T(8,128)S(1)}, f32[12,512,1024]{2,1,0:T(8,128)}) fusion(f32[12,512,1024]{2,1,0:T(8,128)} %fusion.124, f32[12,512]{1,0:T(8,128)S(1)} %dynamic-slice_bitcast_fusion.2, pred[512,1024]{1,0:T(8,128)(4,1)S(1)} %broadcast_compare_fusion.5, bf16[1024,12,64]{0,2,1:T(8,128)(2,1)} %get-tuple-element.510, ...), kind=kOutput, calls=%fused_computation.18.clone.1 | convolution fusion | flops 836757504 | bytes 53264388 | tf_op jit(solution)/shard_map/while/body/eval_jaxpr/qhd,khd->hqk/dot_general | solution.py:152
  467.2 22.4 %multiply_convert_fusion.7 = bf16[12,512,1024]{2,1,0:T(8,128)(2,1)} fusion(f32[12,512,1024]{2,1,0:T(8,128)} %get-tuple-element.445, f32[12,512,1024]{2,1,0:T(8,128)} %fusion.124, f32[12,512]{1,0:T(8,128)S(1)} %get-tuple-element.446, f32[12,512]{1,0:T(8,128)S(1)} %dynamic-slice_bitcast_fusion.2, pred[512,1024]{1,0:T(8,128)(4,1)S(1)} %broadcast_compare_fusion.5), kind=kLoop, calls=%fused_computation.17.clone.1 | loop fusion | flops 37748736 | bytes 63488000 | tf_op jit(solution)/shard_map/while/body/eval_jaxpr/convert_element_type | solution.py:159
  489.6 9.8 %multiply_bitcast_fusion.2 = f32[1,512,12,64]{1,3,2,0:T(8,128)} fusion(bf16[12,512,1024]{2,1,0:T(8,128)(2,1)} %multiply_convert_fusion.7, bf16[1024,12,64]{0,2,1:T(8,128)(2,1)S(1)} %get-tuple-element.507), kind=kOutput, calls=%fused_computation.25.clone.1 | convolution fusion | flops 805699584 | bytes 15728640 | tf_op jit(solution)/shard_map/while/body/eval_jaxpr/hqk,khd->qhd/dot_general | solution.py:161
  499.4 10.0 %bitcast_add_fusion.4 = f32[1024,12,64]{0,2,1:T(8,128)} fusion(f32[1024,12,64]{0,2,1:T(8,128)} %get-tuple-element.488, bf16[12,512,1024]{2,1,0:T(8,128)(2,1)} %multiply_convert_fusion.7, pred[]{:T(512)S(6)} %compare.9, bf16[2,512,12,64]{1,3,2,0:T(8,128)(2,1)} %get-tuple-element.504, s32[]{:T(128)S(6)} %copy.110), kind=kOutput, calls=%fused_computation.24.clone.1 | convolution fusion | flops 807665664 | bytes 19660804 | tf_op jit(solution)/shard_map/while/body/eval_jaxpr/hqk,qhd->khd/dot_general | solution.py:166
  509.3 1.6 copy.90
  511.0 28.7 %dynamic_update_slice.19 = f32[2,512,12,64]{1,0,3,2:T(2,128)} dynamic-update-slice(f32[2,512,12,64]{1,0,3,2:T(2,128)} %get-tuple-element.490, f32[1,512,12,64]{1,0,3,2:T(1,128)S(1)} %copy.90, s32[]{:T(128)S(6)} %copy.110, s32[]{:T(128)} %constant.33.clone.1..sunk, s32[]{:T(128)} %constant.33.clone.1..sunk, s32[]{:T(128)} %constant.33.clone.1..sunk) | dynamic-update-slice | bytes 3145732 | tf_op jit(solution)/shard_map/while/body/jit(dynamic_update_index_in_dim)/dynamic_update_slice | solution.py:106
  539.9 5.8 reshape.259
  545.7 2.8 multiply_add_fusion.4
  549.0 2.2 convert_bitcast_fusion
  551.8 2.2 copy-done.12
  554.0 6.2 fusion.61
  560.9 5.4 multiply_convert_fusion.2
  566.3 1.6 copy.62
  567.9 8.9 %fusion.47 = (f32[1024]{0:T(1024)S(1)}, f32[1024,768]{0,1:T(8,128)}) fusion(bf16[1024,768]{0,1:T(8,128)(2,1)S(1)} %copy-done.3, f32[768]{0:T(1024)S(1)} %copy-done.27, f32[1024]{0:T(1024)S(1)} %copy-done.25, bf16[768,2304]{1,0:T(8,128)(2,1)} %all-gather.5.cloned.1.call-done, bf16[1024,2304]{0,1:T(8,128)(2,1)} %bitcast.137), kind=kOutput, calls=%fused_computation.80 | convolution fusion | flops 3627809792 | bytes 12987392 | tf_op jit(solution)/shard_map/ne,de->nd/dot_general | solution.py:186
  576.9 114.7 %reduce-scatter.5.cloned.1.call-done = f32[96,2304]{1,0:T(8,128)} async-done(((f32[768,2304]{1,0:T(8,128)}), f32[96,2304]{1,0:T(8,128)}) %reduce-scatter.5.cloned.1.call-update) | async-done | bytes 884752 | tf_op jit(solution)/shard_map/reduce_scatter | solution.py:194
  691.6 3.3 fusion.45
  694.9 12.5 %all-reduce.10 = (f32[768]{0:T(1024)S(1)}, f32[768]{0:T(1024)S(1)}) all-reduce(f32[768]{0:T(1024)S(1)} %get-tuple-element.229, f32[768]{0:T(1024)S(1)} %copy-done.37), channel_id=2, replica_groups=mesh['rep'=4,'shard'=8] {'shard'}, use_global_device_ids=true, to_apply=%region_19.20.clone | all-reduce | flops 1536 | bytes 12288
  707.5 5.6 add_convert_fusion.1
  713.2 2.6 copy.63
  715.8 10.0 %all-reduce.11 = (f32[96]{0:T(128)}, f32[96]{0:T(128)}) all-reduce(f32[96]{0:T(128)S(1)} %dynamic-slice.3, f32[96]{0:T(128)S(1)} %dynamic-slice.5), channel_id=1, replica_groups=mesh['rep'=4,'shard'=8] {'rep'}, use_global_device_ids=true, to_apply=%region_20.21 | all-reduce | flops 192 | bytes 1536 | tf_op jit(solution)/shard_map/psum | solution.py:200
  725.7 27.4 %all-reduce.16.cloned.1.call-done = (f32[96,2304]{1,0:T(8,128)}, f32[96,768]{1,0:T(8,128)}, f32[96,2304]{1,0:T(8,128)}, f32[144,768]{1,0:T(8,128)}) async-done(((f32[96,2304]{1,0:T(8,128)}, f32[96,768]{1,0:T(8,128)}, f32[96,2304]{1,0:T(8,128)}, f32[144,768]{1,0:T(8,128)}), (f32[96,2304]{1,0:T(8,128)}, f32[96,768]{1,0:T(8,128)}, f32[96,2304]{1,0:T(8,128)}, ...) | async-done | bytes 2506768 | tf_op jit(solution)/shard_map/psum | solution.py:200
  753.2 2.2 copy.122
  755.4 1.7 copy.123
  757.1 2.1 copy.124
  (160 shorter events, 28.8 us)
Async XLA Ops:
  7.2 67.2 %all-gather.5.cloned.1.call-start = ((), (), s32[]{:S(2)}) async-start(), calls=%async_computation.4 | async-start | bytes 3981312 | tf_op jit(solution)/shard_map/all_gather | solution.py:70
  7.9 158.5 %all-gather.7.cloned.1.call-start = ((), (), s32[]{:S(2)}) async-start(), calls=%async_computation.5 | async-start | bytes 1327104 | tf_op jit(solution)/shard_map/all_gather | solution.py:71
  8.6 173.6 %all-gather.9.cloned.1.call-start = ((), (), s32[]{:S(2)}) async-start(), calls=%async_computation.6 | async-start | bytes 3981312 | tf_op jit(solution)/shard_map/all_gather | solution.py:73
  9.4 220.8 %all-gather.11.cloned.1.call-start = ((), (), s32[]{:S(2)}) async-start(), calls=%async_computation.7 | async-start | bytes 1990656 | tf_op jit(solution)/shard_map/all_gather | solution.py:74
  10.0 566.9 %reduce-scatter.7.cloned.1.call-start = ((), (), s32[]{:S(2)}) async-start(), calls=%async_computation.9 | async-start | bytes 2654208 | tf_op jit(solution)/shard_map/reduce_scatter | solution.py:195
  27.4 46.9 %copy-start.26 = (f32[768]{0:T(1024)}, f32[768]{0:T(1024)S(1)}, u32[]{:S(2)}) copy-start(f32[768]{0:T(1024)S(1)} %convert_element_type.87) | copy-start | bytes 9220
  30.0 3.2 copy-start.13
  31.9 134.5 %copy-start.2 = (bf16[1024,768]{0,1:T(8,128)(2,1)}, bf16[1024,768]{0,1:T(8,128)(2,1)S(1)}, u32[]{:S(2)}) copy-start(bf16[1024,768]{0,1:T(8,128)(2,1)S(1)} %copy.52) | copy-start | bytes 4718596
  32.2 48.5 %copy-start.24 = (f32[1024]{0:T(1024)}, f32[1024]{0:T(1024)S(1)}, u32[]{:S(2)}) copy-start(f32[1024]{0:T(1024)S(1)} %broadcast_multiply_fusion.1) | copy-start | bytes 12292
  32.6 0.6 copy-start.34
  33.3 47.4 %copy-start.30 = (f32[1024]{0:T(1024)}, f32[1024]{0:T(1024)S(1)}, u32[]{:S(2)}) copy-start(f32[1024]{0:T(1024)S(1)} %fusion.66) | copy-start | bytes 12292
  35.5 47.7 %copy-start.19 = (f32[1024,32]{0,1:T(8,128)}, f32[1024,32]{0,1:T(8,128)S(1)}, u32[]{:S(2)}) copy-start(f32[1024,32]{0,1:T(8,128)S(1)} %get-tuple-element.307) | copy-start | bytes 393220
  35.5 47.7 %copy-start.21 = (f32[1024,32]{0,1:T(8,128)}, f32[1024,32]{0,1:T(8,128)S(1)}, u32[]{:S(2)}) copy-start(f32[1024,32]{0,1:T(8,128)S(1)} %get-tuple-element.308) | copy-start | bytes 393220
  99.0 12.0 %copy-start.14 = (bf16[2,512,12,64]{1,3,2,0:T(8,128)(2,1)S(1)}, bf16[2,512,12,64]{1,3,2,0:T(8,128)(2,1)}, u32[]{:S(2)}) copy-start(bf16[2,512,12,64]{1,3,2,0:T(8,128)(2,1)} %get-tuple-element.457) | copy-start | bytes 4718596 | tf_op jit(solution)/shard_map/while
  122.6 1.1 copy-start.15
  136.2 12.0 %copy-start.14 = (bf16[2,512,12,64]{1,3,2,0:T(8,128)(2,1)S(1)}, bf16[2,512,12,64]{1,3,2,0:T(8,128)(2,1)}, u32[]{:S(2)}) copy-start(bf16[2,512,12,64]{1,3,2,0:T(8,128)(2,1)} %get-tuple-element.457) | copy-start | bytes 4718596 | tf_op jit(solution)/shard_map/while
  160.3 1.1 copy-start.15
  169.7 1.6 copy-start.8
  169.7 12.6 %copy-start.36 = (f32[768]{0:T(1024)S(1)}, f32[768]{0:T(1024)}, u32[]{:S(2)}) copy-start(f32[768]{0:T(1024)} %convert_element_type.93) | copy-start | bytes 9220
  171.3 58.9 %copy-start.6 = (bf16[1024,768]{0,1:T(8,128)(2,1)S(1)}, bf16[1024,768]{0,1:T(8,128)(2,1)}, u32[]{:S(2)}) copy-start(bf16[1024,768]{0,1:T(8,128)(2,1)} %copy.58) | copy-start | bytes 4718596
  171.3 58.9 %copy-start.28 = (f32[1024]{0:T(1024)S(1)}, f32[1024]{0:T(1024)}, u32[]{:S(2)}) copy-start(f32[1024]{0:T(1024)} %fusion.65) | copy-start | bytes 12292
  230.2 27.1 %copy-start.10 = (f32[1024,2304]{1,0:T(8,128)S(1)}, f32[1024,2304]{1,0:T(8,128)}, u32[]{:S(2)}) copy-start(f32[1024,2304]{1,0:T(8,128)} %fusion.70) | copy-start | bytes 28311556
  257.3 3.5 copy-start.9
  260.8 9.6 %copy-start.11 = (f32[1024,1152]{1,0:T(8,128)}, f32[1024,1152]{1,0:T(8,128)S(1)}, u32[]{:S(2)}) copy-start(f32[1024,1152]{1,0:T(8,128)S(1)} %get-tuple-element.291) | copy-start | bytes 14155780
  271.2 1.8 copy-start.4
  271.3 1.7 copy-start.32
  271.3 2.9 copy-start.16
  273.0 1.2 copy-start.17
  277.2 299.6 %reduce-scatter.11.cloned.1.call-start = ((), (), s32[]{:S(2)}) async-start(), calls=%async_computation.11 | async-start | bytes 3981312 | tf_op jit(solution)/shard_map/reduce_scatter | solution.py:198
  282.8 1.4 copy-start.18
  282.8 294.1 %reduce-scatter.9.cloned.1.call-start = ((), (), s32[]{:S(2)}) async-start(), calls=%async_computation.10 | async-start | bytes 7962624 | tf_op jit(solution)/shard_map/reduce_scatter | solution.py:197
  306.8 384.7 %reduce-scatter.5.cloned.1.call-start = ((), (), s32[]{:S(2)}) async-start(), calls=%async_computation.8 | async-start | bytes 7962624 | tf_op jit(solution)/shard_map/reduce_scatter | solution.py:194
  307.7 11.6 %copy-start.5 = (bf16[2,512,12,64]{1,3,2,0:T(8,128)(2,1)S(1)}, bf16[2,512,12,64]{1,3,2,0:T(8,128)(2,1)}, u32[]{:S(2)}) copy-start(bf16[2,512,12,64]{1,3,2,0:T(8,128)(2,1)} %get-tuple-element.509) | copy-start | bytes 4718596 | tf_op jit(solution)/shard_map/while
  382.6 9.1 %copy-start.1 = (f32[1,512,12,64]{1,3,2,0:T(8,128)S(1)}, f32[1,512,12,64]{1,3,2,0:T(8,128)}, u32[]{:S(2)}) copy-start(f32[1,512,12,64]{1,3,2,0:T(8,128)} %multiply_bitcast_fusion.2) | copy-start | bytes 4718596 | tf_op jit(solution)/shard_map/while
  422.5 11.5 %copy-start.5 = (bf16[2,512,12,64]{1,3,2,0:T(8,128)(2,1)S(1)}, bf16[2,512,12,64]{1,3,2,0:T(8,128)(2,1)}, u32[]{:S(2)}) copy-start(bf16[2,512,12,64]{1,3,2,0:T(8,128)(2,1)} %get-tuple-element.509) | copy-start | bytes 4718596 | tf_op jit(solution)/shard_map/while
  499.4 10.0 %copy-start.1 = (f32[1,512,12,64]{1,3,2,0:T(8,128)S(1)}, f32[1,512,12,64]{1,3,2,0:T(8,128)}, u32[]{:S(2)}) copy-start(f32[1,512,12,64]{1,3,2,0:T(8,128)} %multiply_bitcast_fusion.2) | copy-start | bytes 4718596 | tf_op jit(solution)/shard_map/while
  539.9 5.8 copy-start
  539.9 5.8 copy-start.20
  539.9 5.8 copy-start.22
  551.2 2.8 copy-start.3
  551.2 2.8 copy-start.25
  551.2 2.8 copy-start.27
  551.2 2.8 copy-start.31
  551.8 2.2 copy-start.12
  560.2 0.7 copy-start.29
  560.2 193.0 %all-reduce.16.cloned.1.call-start = ((), (), s32[]{:S(2)}) async-start(), calls=%async_computation.12 | async-start | bytes 5013504 | tf_op jit(solution)/shard_map/psum | solution.py:200
  567.9 8.9 %copy-start.35 = (f32[1024]{0:T(1024)S(1)}, f32[1024]{0:T(1024)}, u32[]{:S(2)}) copy-start(f32[1024]{0:T(1024)} %copy-done.34) | copy-start | bytes 12292
  691.6 3.3 copy-start.37
  691.6 16.0 %copy-start.7 = (bf16[1024,768]{0,1:T(8,128)(2,1)S(1)}, bf16[1024,768]{0,1:T(8,128)(2,1)}, u32[]{:S(2)}) copy-start(bf16[1024,768]{0,1:T(8,128)(2,1)} %copy.58) | copy-start | bytes 4718596
  691.6 16.0 %copy-start.33 = (f32[1024]{0:T(1024)S(1)}, f32[1024]{0:T(1024)}, u32[]{:S(2)}) copy-start(f32[1024]{0:T(1024)} %copy-done.32) | copy-start | bytes 12292
  753.2 6.0 copy-start.23
Sparse Core Ops, SparseCore 0:
  10.2 64.1 all-gather.4
  76.5 39.6 all-gather.6
  118.4 63.8 all-gather.8
  184.3 45.8 all-gather.10
  277.3 66.5 reduce-scatter.6
  347.5 80.6 reduce-scatter.10
  431.8 127.4 reduce-scatter.8
  563.5 128.0 reduce-scatter.4
  694.2 58.9 all-reduce.15
where the time goes:
time: 774 us; the launch traced here: 767 us
  matrix products  276 us (36%)
  waiting for transfers between devices  232 us (30%)
  local copies, waits for them, and re-layouts  111 us (14%)
  other arithmetic  96 us (12%)
  blocking collectives  34.8 us (4%)
  between operations  15.8 us (2%)
    reduce_scatter x1, waiting for transfers between devices, per_device(): lax.psum_scatter(grad_qkv_w, 'shard', scatter_dimension=0, tiled=True)  115 us
    dynamic_update_slice x4, local copies, waits for them, and re-layouts, per_device(): attended, log_totals = lax.map(forward_block, (query_blocks, seg_blocks))  60.7 us
    dot_general x4, matrix products, block_scores(): jnp.einsum('qhd,khd->hqk', query_block, keys_rot, preferred_element_type=...  47.1 us
    convert_element_type x2, other arithmetic, backward_block(): grad_scores = (prob_f32 * (grad_prob - row_delta)).astype(jnp.bfloat16)  44.2 us
    all_gather x1, waiting for transfers between devices, per_device(): lax.all_gather(qkv_weight, 'shard', axis=0, tiled=True)  38.8 us
    all_gather x1, waiting for transfers between devices, per_device(): lax.all_gather(mlp_out_weight, 'shard', axis=0, tiled=True)  37.3 us
    dot_general x2, matrix products, backward_block(): jnp.einsum('qhd,khd->hqk', grad_block, values_low, preferred_element_type...  36.4 us
    unnamed x86, local copies, waits for them, and re-layouts  30.7 us
  transfers between devices with their start and end apart: 9, of which 5 were waited for; matrix products, arithmetic and copies ran while one was open for 55% of the time, Pallas kernels for 0%

commit v1 on v0

v1 whole, which is shorter than its diff:
```python
import functools

import jax
import jax.numpy as jnp
from jax import lax
from jax.experimental import pallas as pl
from jax.experimental.pallas import tpu as pltpu
from jax.sharding import PartitionSpec as P

HEADS = 12


rope_base = 160000.0
norm_eps = 1e-05
masked_score = -1000000000.0
log2e = 1.4426950408889634
MIB = 1024 * 1024


def layer_norm(values, gain_vec):
    centered = values - jnp.mean(values, axis=-1, keepdims=True)
    spread = jnp.mean(centered * centered, axis=-1, keepdims=True)
    return centered * lax.rsqrt(spread + norm_eps) * gain_vec


def rotary_tables(lengths, token_rows, head_width):
    seq_ends = jnp.cumsum(lengths)
    row_ids = jnp.arange(token_rows, dtype=jnp.int32)
    passed = row_ids[:, None] >= seq_ends[None, :]
    segment = jnp.sum(passed.astype(jnp.int32), axis=1)
    starts = jnp.sum(jnp.where(passed, lengths[None, :], 0), axis=1)
    position = (row_ids - starts).astype(jnp.float32)
    half_width = head_width // 2
    frequency = rope_base ** (-(jnp.arange(half_width, dtype=jnp.float32) * 2.0 / head_width))
    angles = position[:, None] * frequency[None, :]
    valid_rows = (row_ids < seq_ends[-1]).astype(jnp.float32)
    return (jnp.cos(angles), jnp.sin(angles), segment, valid_rows)


def geglu(gate_up):
    hidden_units = gate_up.shape[-1] // 2
    return jax.nn.gelu(gate_up[:, :hidden_units], approximate=False) * gate_up[:, hidden_units:]


def nn(a, b):
    return jnp.dot(a, b, preferred_element_type=jnp.float32)


def nt(a, b):
    return lax.dot_general(a, b, (((1,), (1,)), ((), ())), preferred_element_type=jnp.float32)


def rotate(values, cos_wide, sin_wide):
    lane = lax.broadcasted_iota(jnp.int32, values.shape, 1)
    width = values.shape[1]
    swapped = jnp.where(
        (lane & 32) == 0, pltpu.roll(values, width - 32, 1), pltpu.roll(values, 32, 1)
    )
    return values * cos_wide + swapped * sin_wide


QB = 256


def attn_fwd_kernel(scale, a_ref, w_ref, cos_ref, sin_ref, segc_ref, segr_ref, qkv_ref, o_ref, lse_ref):
    rows = a_ref.shape[0]
    a1 = a_ref[...]
    cos_wide, sin_wide = cos_ref[...], sin_ref[...]
    q = rotate(nn(a1, w_ref[0]), cos_wide, sin_wide).astype(jnp.bfloat16)
    k = rotate(nn(a1, w_ref[1]), cos_wide, sin_wide).astype(jnp.bfloat16)
    v = nn(a1, w_ref[2])
    qkv_ref[0] = q
    qkv_ref[1] = k
    qkv_ref[2] = v.astype(jnp.bfloat16)
    v_t = jnp.transpose(v).astype(jnp.bfloat16)
    segc = segc_ref[...]
    ones = jnp.ones((16, rows), jnp.bfloat16)
    for b in range(rows // QB):
        qs = slice(b * QB, (b + 1) * QB)
        same = segc == segr_ref[:, qs]
        outs = []
        for h in range(2):
            hs = slice(h * 64, (h + 1) * 64)
            s_t = nt(k[:, hs], q[qs, hs]) * (scale * log2e)
            s_t = jnp.where(same, s_t, masked_score)
            top = jnp.max(s_t, axis=0, keepdims=True)
            e = jnp.exp2(s_t - top).astype(jnp.bfloat16)
            ov = nn(jnp.concatenate([v_t[hs], ones], axis=0), e)
            total = ov[64:65]
            outs.append(ov[:64] * (1.0 / total))
            lse_ref[0, h : h + 1, qs] = top + jnp.log2(total)
        o_ref[qs, :] = jnp.transpose(jnp.concatenate(outs, axis=0)).astype(jnp.bfloat16)


def attn_bwd_kernel(scale, qkv_ref, o_ref, go_ref, lse_ref, cos_ref, sin_ref, segc_ref, segr_ref, g_ref):
    rows = o_ref.shape[0]
    q, k, v, go = qkv_ref[0], qkv_ref[1], qkv_ref[2], go_ref[...]
    k_t = jnp.transpose(k.astype(jnp.float32)).astype(jnp.bfloat16)
    prod = jnp.transpose(go.astype(jnp.float32) * o_ref[...].astype(jnp.float32))
    segc = segc_ref[...]
    gk = [jnp.zeros((rows, 64), jnp.float32) for _ in range(2)]
    gv = [jnp.zeros((rows, 64), jnp.float32) for _ in range(2)]
    gq = []
    for b in range(rows // QB):
        qs = slice(b * QB, (b + 1) * QB)
        same = segc == segr_ref[:, qs]
        outs = []
        for h in range(2):
            hs = slice(h * 64, (h + 1) * 64)
            delta = jnp.sum(prod[hs, qs], axis=0, keepdims=True)
            s_t = nt(k[:, hs], q[qs, hs]) * (scale * log2e)
            p = jnp.exp2(jnp.where(same, s_t - lse_ref[0, h : h + 1, qs], masked_score))
            gp = nt(v[:, hs], go[qs, hs])
            gv[h] = gv[h] + nn(p.astype(jnp.bfloat16), go[qs, hs])
            ds = (p * (gp - delta)).astype(jnp.bfloat16)
            gk[h] = gk[h] + nn(ds, q[qs, hs])
            outs.append(nn(k_t[hs], ds))
        gq.append(jnp.transpose(jnp.concatenate(outs, axis=0)))
    cos_wide, sin_wide = cos_ref[...], sin_ref[...]
    gq = jnp.concatenate(gq, axis=0) * scale
    gk = jnp.concatenate(gk, axis=1) * scale
    g_ref[0] = rotate(gq, cos_wide, -sin_wide).astype(jnp.bfloat16)
    g_ref[1] = rotate(gk, cos_wide, -sin_wide).astype(jnp.bfloat16)
    g_ref[2] = jnp.concatenate(gv, axis=1).astype(jnp.bfloat16)


def whole_spec(shape):
    return pl.BlockSpec(shape, lambda i: tuple(0 for _ in shape))


def attn_forward(a1, w_qkv, cos_wide, sin_wide, segc, segr):
    rows, width = a1.shape
    pairs = HEADS // 2
    return pl.pallas_call(
        functools.partial(attn_fwd_kernel, (width // HEADS) ** (-0.5)),
        grid=(pairs,),
        in_specs=[
            whole_spec((rows, width)),
            pl.BlockSpec((3, width, 128), lambda i: (0, 0, i)),
            whole_spec((rows, 128)),
            whole_spec((rows, 128)),
            whole_spec((rows, 1)),
            whole_spec((1, rows)),
        ],
        out_specs=[
            pl.BlockSpec((3, rows, 128), lambda i: (0, 0, i)),
            pl.BlockSpec((rows, 128), lambda i: (0, i)),
            pl.BlockSpec((1, 2, rows), lambda i: (i, 0, 0)),
        ],
        out_shape=[
            jax.ShapeDtypeStruct((3, rows, width), jnp.bfloat16),
            jax.ShapeDtypeStruct((rows, width), jnp.bfloat16),
            jax.ShapeDtypeStruct((pairs, 2, rows), jnp.float32),
        ],
        compiler_params=pltpu.CompilerParams(vmem_limit_bytes=50 * MIB),
        cost_estimate=pl.CostEstimate(
            flops=2 * rows * rows * width * 2 + 6 * rows * width * width,
            bytes_accessed=20 * MIB,
            transcendentals=HEADS * rows * rows,
        ),
    )(a1, w_qkv, cos_wide, sin_wide, segc, segr)


def attn_backward(qkv, o, go, lse, cos_wide, sin_wide, segc, segr):
    rows, width = o.shape
    pairs = HEADS // 2
    pair_block = pl.BlockSpec((rows, 128), lambda i: (0, i))
    return pl.pallas_call(
        functools.partial(attn_bwd_kernel, (width // HEADS) ** (-0.5)),
        grid=(pairs,),
        in_specs=[
            pl.BlockSpec((3, rows, 128), lambda i: (0, 0, i)),
            pair_block,
            pair_block,
            pl.BlockSpec((1, 2, rows), lambda i: (i, 0, 0)),
            whole_spec((rows, 128)),
            whole_spec((rows, 128)),
            whole_spec((rows, 1)),
            whole_spec((1, rows)),
        ],
        out_specs=pl.BlockSpec((3, rows, 128), lambda i: (0, 0, i)),
        out_shape=jax.ShapeDtypeStruct((3, rows, width), jnp.bfloat16),
        compiler_params=pltpu.CompilerParams(vmem_limit_bytes=50 * MIB),
        cost_estimate=pl.CostEstimate(
            flops=2 * rows * rows * width * 5,
            bytes_accessed=20 * MIB,
            transcendentals=HEADS * rows * rows,
        ),
    )(qkv, o, go, lse, cos_wide, sin_wide, segc, segr)


def gather_weights(norm1_scale, qkv_weight, out_weight, norm2_scale, in_weight, mlp_out_weight):
    gather = functools.partial(lax.all_gather, axis_name="shard", axis=0, tiled=True)
    w_qkv = gather(qkv_weight)
    width = w_qkv.shape[0]
    w_qkv = w_qkv.reshape(width, 3, width).transpose(1, 0, 2)
    return (
        gather(norm1_scale),
        w_qkv,
        gather(out_weight),
        gather(norm2_scale),
        gather(in_weight),
        gather(mlp_out_weight),
    )


def reduce_grads(grads):
    def one(grad):
        part = lax.psum_scatter(
            grad.astype(jnp.bfloat16), "shard", scatter_dimension=0, tiled=True
        )
        return lax.psum(part, "rep").astype(jnp.float32)

    g1, gqkv, gout, g2, gin, gmlp = grads
    width = gout.shape[0]
    gqkv = gqkv.transpose(1, 0, 2).reshape(width, 3 * width)
    return tuple(one(item) for item in (g1, gqkv, gout, g2, gin, gmlp))


def per_device(
    hidden_in,
    seq_lengths,
    norm1_scale,
    qkv_weight,
    out_weight,
    norm2_scale,
    in_weight,
    mlp_out_weight,
    cotangent,
):
    token_rows, model_width = hidden_in.shape
    head_width = model_width // HEADS
    cosine, sine, segment, valid_rows = rotary_tables(seq_lengths[0], token_rows, head_width)
    cos_wide = jnp.concatenate([cosine] * 4, axis=1)
    sin_wide = jnp.concatenate([-sine, sine] * 2, axis=1)
    segc, segr = segment[:, None], segment[None, :]
    gain1, w_qkv, w_out, gain2, w_in, w_mlp = gather_weights(
        norm1_scale, qkv_weight, out_weight, norm2_scale, in_weight, mlp_out_weight
    )
    gain1, gain2 = gain1.astype(jnp.float32), gain2.astype(jnp.float32)
    inputs_f32 = hidden_in.astype(jnp.float32)
    normed_one, norm_one_back = jax.vjp(layer_norm, inputs_f32, gain1)
    normed_one = normed_one.astype(jnp.bfloat16)
    qkv, attn_low, lse = attn_forward(normed_one, w_qkv, cos_wide, sin_wide, segc, segr)
    resid_one = inputs_f32 + nn(attn_low, w_out)
    normed_two, norm_two_back = jax.vjp(layer_norm, resid_one, gain2)
    normed_two = normed_two.astype(jnp.bfloat16)
    gate_up = nn(normed_two, w_in)
    mixed, geglu_back = jax.vjp(geglu, gate_up)
    mixed_low = mixed.astype(jnp.bfloat16)
    output = (valid_rows[:, None] * (resid_one + nn(mixed_low, w_mlp))).astype(jnp.bfloat16)

    cot_rows = cotangent.astype(jnp.float32) * valid_rows[:, None]
    mlp_cot = cot_rows.astype(jnp.bfloat16)
    grad_mlp_out = jnp.einsum("nf,nd->fd", mixed_low, mlp_cot, preferred_element_type=jnp.float32)
    grad_mixed = nt(mlp_cot, w_mlp)
    grad_gate_up = geglu_back(grad_mixed)[0].astype(jnp.bfloat16)
    grad_in_w = jnp.einsum(
        "nd,nf->df", normed_two, grad_gate_up, preferred_element_type=jnp.float32
    )
    grad_normed_two = nt(grad_gate_up, w_in)
    grad_resid_ln, grad_gain_two = norm_two_back(grad_normed_two)
    grad_resid = cot_rows + grad_resid_ln
    attn_cot = grad_resid.astype(jnp.bfloat16)
    grad_out_w = jnp.einsum("nd,ne->de", attn_low, attn_cot, preferred_element_type=jnp.float32)
    grad_attn = nt(attn_cot, w_out).astype(jnp.bfloat16)
    grad_qkv = attn_backward(qkv, attn_low, grad_attn, lse, cos_wide, sin_wide, segc, segr)
    grad_qkv_w = jnp.einsum(
        "nd,cne->cde", normed_one, grad_qkv, preferred_element_type=jnp.float32
    )
    grad_normed_one = jnp.einsum(
        "cne,cde->nd", grad_qkv, w_qkv, preferred_element_type=jnp.float32
    )
    grad_input_ln, grad_gain_one = norm_one_back(grad_normed_one)
    input_grad = (grad_resid + grad_input_ln).astype(jnp.bfloat16)
    owned = reduce_grads(
        (grad_gain_one, grad_qkv_w, grad_out_w, grad_gain_two, grad_in_w, grad_mlp_out)
    )
    return (output, input_grad) + owned


def solution(mesh):
    rows = P(("rep", "shard"), None)
    weights = (P("shard"), P("shard", None), P("shard", None), P("shard"), P("shard", None), P("shard", None))
    return jax.shard_map(
        per_device,
        mesh=mesh,
        in_specs=(rows, rows) + weights + (rows,),
        out_specs=(rows, rows) + weights,
        check_vma=False,
    )
```

time: 774 us -> 628 us (0.81)
  matrix products: 276 us -> 83.4 us
  waiting for transfers between devices: 232 us -> 351 us
  local copies, waits for them, and re-layouts: 111 us -> 24 us
  Pallas kernels: 0 us -> 80.2 us
  other arithmetic: 96 us -> 32.6 us
    dot_general x23 -> x8, matrix products: 256 us -> 64.7 us  [the longest x3 28.8 us: nt(): lax.dot_general(a, b, (((1,), (1,)), ((), ())), preferred_element_type=jn...]
    pallas_call x0 -> x2, Pallas kernels: none -> 80.2 us  [the longest x1 42 us: attn_forward(): pl.pallas_call(functools.partial(attn_fwd_kernel, (width // HEADS) ** (-0...]
    reduce_scatter x4, waiting for transfers between devices: 115 us -> 187 us  [one(): lax.psum_scatter(grad.astype(jnp.bfloat16), 'shard', scatter_dimension=0,...]
    dynamic_update_slice x4 -> x0, local copies, waits for them, and re-layouts: 60.7 us -> none  [per_device(): attended, log_totals = lax.map(forward_block, (query_blocks, seg_blocks))]
    all_gather x4, waiting for transfers between devices: 87.1 us -> 127 us  [the longest x1 48.5 us: gather_weights(): gather(in_weight)]
    convert_element_type x4 -> x9, other arithmetic: 44.8 us -> 10 us  [the longest x6 8.36 us: one(): return lax.psum(part, 'rep').astype(jnp.float32)]
    reduce_sum x3 -> x1, other arithmetic: 24.7 us -> 0.09 us  [rotary_tables(): segment = jnp.sum(passed.astype(jnp.int32), axis=1)]
    unnamed x86 -> x51, local copies, waits for them, and re-layouts: 30.7 us -> 7.35 us
  transfers between devices with their start and end apart: 9 -> 9, of which waited for: 5 -> 7; matrix products, arithmetic and copies ran while one was open for 55% -> 14% of each run, Pallas kernels for 0% -> 13%
where the time goes in v1:
time: 628 us; the launch traced here: 622 us
  waiting for transfers between devices  351 us (56%)
  matrix products  83.4 us (13%)
  Pallas kernels  80.2 us (13%)
  blocking collectives  34.6 us (6%)
  other arithmetic  32.6 us (5%)
  local copies, waits for them, and re-layouts  24 us (4%)
  between operations  15.8 us (3%)
    reduce_scatter x4, waiting for transfers between devices, one(): lax.psum_scatter(grad.astype(jnp.bfloat16), 'shard', scatter_dimension=0,...  187 us
    all_gather x1, waiting for transfers between devices, gather_weights(): gather(in_weight)  48.5 us
    pallas_call x1, Pallas kernels, attn_forward(): pl.pallas_call(functools.partial(attn_fwd_kernel, (width // HEADS) ** (-0...  42 us
    all_gather x1, waiting for transfers between devices, gather_weights(): w_qkv = gather(qkv_weight)  41.1 us
    pallas_call x1, Pallas kernels, attn_backward(): pl.pallas_call(functools.partial(attn_bwd_kernel, (width // HEADS) ** (-0...  38.3 us
    all_gather x1, waiting for transfers between devices, gather_weights(): gather(mlp_out_weight)  37.3 us
    psum x1, waiting for transfers between devices, one(): return lax.psum(part, 'rep').astype(jnp.float32)  35 us
    dot_general x3, matrix products, nt(): lax.dot_general(a, b, (((1,), (1,)), ((), ())), preferred_element_type=jn...  28.8 us
  transfers between devices with their start and end apart: 9, of which 7 were waited for; matrix products, arithmetic and copies ran while one was open for 14% of the time, Pallas kernels for 13%

profile of v1, /device:TPU:11, one launch (start us, length us, event | category | flops | bytes accessed | tf_op | source)
XLA Modules:
  0.0 622.4 jit_solution(5215892519655240679)
XLA Ops:
  7.2 0.7 all-gather.5.cloned.1.call-update
  8.0 0.7 all-gather.7.cloned.1.call-update
  8.7 0.7 all-gather.9.cloned.1.call-update
  9.5 0.5 all-gather.11.cloned.1.call-update
  10.0 1.7 convert_reduce_fusion
  11.8 0.6 fusion.15
  12.4 0.2 reduce-window.4
  12.6 0.1 convert_reduce_fusion.1
  12.7 1.9 fusion.25
  14.6 0.9 pad_maximum_fusion
  15.5 0.6 slice.10
  16.1 0.6 fusion.37
  17.4 0.2 dynamic-update-slice
  17.6 0.2 dynamic-update-slice.1
  17.9 12.9 %all-reduce.7 = (bf16[768]{0:T(1024)(128)(2,1)S(1)}, bf16[768]{0:T(1024)(128)(2,1)S(1)}) all-reduce(bf16[768]{0:T(1024)(128)(2,1)S(1)} %dynamic-update-slice, bf16[768]{0:T(1024)(128)(2,1)S(1)} %dynamic-update-slice.1), channel_id=1, replica_groups=mesh['rep'=4,'shard'=8] {'shard'}, use_global_device_ids=true, to_apply=%add.2 | all-reduce | flops 1536 | bytes 6144
  30.8 0.2 copy.60.segc_ref
  31.0 0.7 fusion.26
  31.7 1.7 fusion.13.a_ref
  33.4 41.1 %all-gather.5.cloned.1.call-done = bf16[768,2304]{1,0:T(8,128)(2,1)} async-done(((bf16[96,2304]{1,0:T(8,128)(2,1)}), bf16[768,2304]{1,0:T(8,128)(2,1)}) %all-gather.5.cloned.1.call-update) | async-done | bytes 3538960 | tf_op jit(solution)/shard_map/all_gather | solution.py:194
  74.5 5.8 copy.57
  80.2 6.1 copy.58
  86.3 42.0 %shard_map.152 = (bf16[3,1024,768]{2,1,0:T(8,128)(2,1)}, bf16[1024,768]{1,0:T(8,128)(2,1)S(1)}, f32[6,2,1024]{2,1,0:T(2,128)S(1)}) custom-call(bf16[1024,768]{1,0:T(8,128)(2,1)} %fusion.13.a_ref, bf16[3,768,768]{2,1,0:T(8,128)(2,1)} %bitcast.49, f32[1024,128]{1,0:T(8,128)S(1)} %get-tuple-element.47.cos_ref, f32[1024,128]{1,0:T(8,128)S(1)} %get-tuple-element.48.sin_ref, ...), custom_call_target="tpu_custom_call" | custom-call | flops 6845104128 | bytes 20971520 | tf_op jit(solution)/shard_map/pallas_call | solution.py:134
  128.2 3.5 fusion.38
  131.7 1.7 copy-done.2
  133.4 0.5 multiply_reduce_fusion.2
  134.0 48.5 %all-gather.9.cloned.1.call-done = bf16[768,2304]{1,0:T(8,128)(2,1)} async-done(((bf16[96,2304]{1,0:T(8,128)(2,1)}), bf16[768,2304]{1,0:T(8,128)(2,1)}) %all-gather.9.cloned.1.call-update) | async-done | bytes 3538960 | tf_op jit(solution)/shard_map/all_gather | solution.py:202
  182.5 10.6 %fusion.34 = f32[1024,2304]{1,0:T(8,128)} fusion(bf16[768,2304]{1,0:T(8,128)(2,1)} %all-gather.9.cloned.1.call-done, f32[1024,768]{1,0:T(8,128)} %copy-done.2, f32[768]{0:T(1024)S(1)} %convert_element_type.101, f32[1024]{0:T(1024)S(1)} %fusion.28, f32[1024]{0:T(1024)S(1)} %broadcast_multiply_fusion), kind=kOutput, calls=%fused_computation.82 | convolution fusion | flops 3627024384 | bytes 16133120 | tf_op jit(solution)/shard_map/dot_general | solution.py:46
  193.0 37.3 %all-gather.11.cloned.1.call-done = bf16[1152,768]{1,0:T(8,128)(2,1)} async-done(((bf16[144,768]{1,0:T(8,128)(2,1)}), bf16[1152,768]{1,0:T(8,128)(2,1)}) %all-gather.11.cloned.1.call-update) | async-done | bytes 1769488 | tf_op jit(solution)/shard_map/all_gather | solution.py:203
  230.4 15.7 %fusion.20 = (f32[1024,1152]{1,0:T(8,128)S(1)}, f32[1024,1152]{1,0:T(8,128)}, f32[1024,1152]{1,0:T(8,128)}) fusion(f32[1024,2304]{1,0:T(8,128)} %fusion.34, bf16[1152,768]{1,0:T(8,128)(2,1)} %all-gather.11.cloned.1.call-done, bf16[1024,768]{1,0:T(8,128)(2,1)} %param.17, f32[1024]{0:T(1024)S(1)} %fusion.26), kind=kOutput, calls=%fused_computation.52 | convolution fusion | flops 1890975744 | bytes 22220800 | tf_op jit(solution)/shard_map/dot_general | solution.py:50
  246.1 7.8 %multiply_add_fusion = (f32[1024,1152]{1,0:T(8,128)S(1)}, bf16[1024,1152]{1,0:T(8,128)(2,1)}) fusion(f32[1024,1152]{1,0:T(8,128)} %get-tuple-element.33, f32[1024,1152]{1,0:T(8,128)} %get-tuple-element.43, f32[1024,2304]{1,0:T(8,128)S(1)} %copy-done.7), kind=kLoop, calls=%fused_computation.13 | loop fusion | flops 20054016 | bytes 25952256 | tf_op jit(solution)/shard_map/transpose(jvp())/add_any | solution.py:42
  253.9 8.6 %multiply_reduce_fusion = (bf16[768]{0:T(1024)(128)(2,1)}, f32[1024]{0:T(1024)S(1)}, f32[1024,768]{1,0:T(8,128)S(1)}) fusion(f32[1024,768]{1,0:T(8,128)S(1)} %copy-done.3, f32[1024]{0:T(1024)S(1)} %fusion.28, f32[1024]{0:T(1024)S(1)} %broadcast_multiply_fusion, f32[768]{0:T(1024)S(1)} %convert_element_type.101, ...), kind=kOutput, calls=%fused_computation.38 | convolution fusion | flops 3634100480 | bytes 19284480 | tf_op jit(solution)/shard_map/dot_general | solution.py:50
  262.6 1.5 fusion.35
  264.1 0.5 fusion.18
  264.7 1.0 copy-done.4
  265.7 1.1 copy-done.12
  266.9 2.5 convolution_convert_fusion.4
  269.4 5.5 convolution_convert_fusion.1
  275.0 0.0 reduce-scatter.9.cloned.1.call-start
  275.0 10.6 %convolution_convert_fusion = bf16[768,2304]{1,0:T(8,128)(2,1)} fusion(f32[1024,1152]{1,0:T(8,128)} %copy-done.5, f32[1024,1152]{1,0:T(8,128)} %copy-done.10, f32[1024,768]{1,0:T(8,128)} %copy-done.2, f32[768]{0:T(1024)S(1)} %convert_element_type.101, f32[1024]{0:T(1024)S(1)} %fusion.28, f32[1024]{0:T(1024)S(1)} %broadcast_multiply_fusion), kind=kOutput, calls=%fused_computation.2 | convolution fusion | flops 3633512448 | bytes 16133120 | tf_op jit(solution)/shard_map/nd,nf->df/dot_general | solution.py:258
  285.7 0.2 reduce-scatter.5.cloned.1.call-start
  285.9 4.4 convolution_convert_fusion.3.go_ref
  290.3 38.3 %shard_map.153 = bf16[3,1024,768]{2,1,0:T(8,128)(2,1)} custom-call(bf16[3,1024,768]{2,1,0:T(8,128)(2,1)} %get-tuple-element.12.qkv_ref, bf16[1024,768]{1,0:T(8,128)(2,1)S(1)} %get-tuple-element.11.o_ref, bf16[1024,768]{1,0:T(8,128)(2,1)} %convolution_convert_fusion.3.go_ref, f32[6,2,1024]{2,1,0:T(2,128)S(1)} %get-tuple-element.13.lse_ref, ...), custom_call_target="tpu_custom_call" | custom-call | flops 8053063680 | bytes 20971520 | tf_op jit(solution)/shard_map/pallas_call | solution.py:168
  328.6 8.3 %convolution_convert_fusion.2 = bf16[768,3,768]{0,2,1:T(8,128)(2,1)S(1)} fusion(bf16[3,1024,768]{2,1,0:T(8,128)(2,1)} %shard_map.153, bf16[1024,768]{1,0:T(8,128)(2,1)S(1)} %copy-done.11), kind=kOutput, calls=%fused_computation.47 | convolution fusion | flops 3625648128 | bytes 9830400 | tf_op jit(solution)/shard_map/nd,cne->cde/dot_general | solution.py:268
  336.9 4.0 copy.67
  341.7 0.6 copy-done.1
  342.3 7.2 %fusion.16 = (f32[1024]{0:T(1024)S(1)}, f32[1024,768,1]{1,0,2:T(8,128)S(1)}) fusion(bf16[1024,768]{1,0:T(8,128)(2,1)S(1)} %copy-done.1, f32[768]{0:T(1024)S(1)} %convert_element_type.97, f32[1024]{0:T(1024)S(1)} %broadcast_multiply_fusion.1, bf16[3,1024,768]{2,1,0:T(8,128)(2,1)} %shard_map.153, bf16[768,3,768]{2,0,1:T(8,128)(2,1)} %copy.58), kind=kOutput, calls=%fused_computation.36 | convolution fusion | flops 3627809792 | bytes 12987392 | tf_op jit(solution)/shard_map/cne,cde->nd/dot_general | solution.py:271
  349.6 1.6 copy-done.6
  351.1 1.7 fusion.14
  352.8 12.9 %all-reduce.6 = (bf16[768]{0:T(1024)(128)(2,1)S(1)}, bf16[768]{0:T(1024)(128)(2,1)S(1)}) all-reduce(bf16[768]{0:T(1024)(128)(2,1)S(1)} %get-tuple-element.16, bf16[768]{0:T(1024)(128)(2,1)S(1)} %copy-done.18), channel_id=2, replica_groups=mesh['rep'=4,'shard'=8] {'shard'}, use_global_device_ids=true, to_apply=%region_12.13.clone | all-reduce | flops 1536 | bytes 6144
  365.8 0.1 dynamic-slice.3
  365.8 0.1 dynamic-slice.5
  365.9 8.8 %all-reduce.8 = (bf16[96]{0:T(256)(128)(2,1)S(1)}, bf16[96]{0:T(256)(128)(2,1)S(1)}) all-reduce(bf16[96]{0:T(256)(128)(2,1)S(1)} %dynamic-slice.3, bf16[96]{0:T(256)(128)(2,1)S(1)} %dynamic-slice.5), channel_id=1, replica_groups=mesh['rep'=4,'shard'=8] {'rep'}, use_global_device_ids=true, to_apply=%region_13.14 | all-reduce | flops 192 | bytes 768 | tf_op jit(solution)/shard_map/psum | solution.py:212
  374.7 0.5 convert_element_type.112
  375.2 0.5 convert_element_type.119
  375.7 4.5 add_convert_fusion.1
  380.3 20.4 %reduce-scatter.11.cloned.1.call-done = bf16[144,768]{1,0:T(8,128)(2,1)} async-done(((bf16[1152,768]{1,0:T(8,128)(2,1)}), bf16[144,768]{1,0:T(8,128)(2,1)}) %reduce-scatter.11.cloned.1.call-update) | async-done | bytes 221200 | tf_op jit(solution)/shard_map/reduce_scatter | solution.py:209
  400.6 83.6 %reduce-scatter.9.cloned.1.call-done = bf16[96,2304]{1,0:T(8,128)(2,1)} async-done(((bf16[768,2304]{1,0:T(8,128)(2,1)}), bf16[96,2304]{1,0:T(8,128)(2,1)}) %reduce-scatter.9.cloned.1.call-update) | async-done | bytes 442384 | tf_op jit(solution)/shard_map/reduce_scatter | solution.py:209
  484.2 82.6 %reduce-scatter.5.cloned.1.call-done = bf16[96,2304]{1,0:T(8,128)(2,1)} async-done(((bf16[768,2304]{1,0:T(8,128)(2,1)}), bf16[96,2304]{1,0:T(8,128)(2,1)}) %reduce-scatter.5.cloned.1.call-update) | async-done | bytes 442384 | tf_op jit(solution)/shard_map/reduce_scatter | solution.py:209
  566.9 6.5 %multiply_convert_fusion.1 = bf16[1024,768]{1,0:T(8,128)(2,1)} fusion(f32[1024,768]{1,0:T(8,128)} %copy-done.2, bf16[1024,1152]{1,0:T(8,128)(2,1)} %get-tuple-element.35, bf16[1152,768]{1,0:T(8,128)(2,1)} %all-gather.11.cloned.1.call-done, f32[1024]{0:T(1024)S(1)} %fusion.26), kind=kOutput, calls=%fused_computation.44 | convolution fusion | flops 1814298624 | bytes 8851456 | tf_op jit(solution)/shard_map/dot_general | solution.py:46
  573.3 35.0 %all-reduce.12.cloned.1.call-done = (bf16[96,2304]{1,0:T(8,128)(2,1)}, bf16[96,768]{1,0:T(8,128)(2,1)}, bf16[96,2304]{1,0:T(8,128)(2,1)}, bf16[144,768]{1,0:T(8,128)(2,1)}) async-done(((bf16[96,2304]{1,0:T(8,128)(2,1)}, bf16[96,768]{1,0:T(8,128)(2,1)}, bf16[96,2304]{1,0:T(8,128)(2,1)}, bf16[144,768]{1,0:T(8,128)(2,1)}), (bf16[96,2304]{1,0:T(8,128)(2,1)}, bf16[96,768]{1,0:T(8,128)(2,1)}, ...) | async-done | bytes 1253392 | tf_op jit(solution)/shard_map/psum | solution.py:212
  608.4 1.6 convert_element_type.117
  610.0 2.0 convert_element_type.115
  612.0 1.7 convert_element_type.123
  613.7 2.0 convert_element_type.121
  (67 shorter events, 0.5 us)
Async XLA Ops:
  7.2 4.6 copy-start
  7.2 5.3 copy-start.19
  7.2 67.3 %all-gather.5.cloned.1.call-start = ((), (), s32[]{:S(2)}) async-start(), calls=%async_computation.4 | async-start | bytes 3981312 | tf_op jit(solution)/shard_map/all_gather | solution.py:194
  7.9 120.3 %all-gather.7.cloned.1.call-start = ((), (), s32[]{:S(2)}) async-start(), calls=%async_computation.5 | async-start | bytes 1327104 | tf_op jit(solution)/shard_map/all_gather | solution.py:200
  8.7 173.8 %all-gather.9.cloned.1.call-start = ((), (), s32[]{:S(2)}) async-start(), calls=%async_computation.6 | async-start | bytes 3981312 | tf_op jit(solution)/shard_map/all_gather | solution.py:202
  9.4 221.0 %all-gather.11.cloned.1.call-start = ((), (), s32[]{:S(2)}) async-start(), calls=%async_computation.7 | async-start | bytes 1990656 | tf_op jit(solution)/shard_map/all_gather | solution.py:203
  10.0 370.3 %reduce-scatter.7.cloned.1.call-start = ((), (), s32[]{:S(2)}) async-start(), calls=%async_computation.9 | async-start | bytes 1327104 | tf_op jit(solution)/shard_map/reduce_scatter | solution.py:209
  11.7 4.4 copy-start.17
  11.7 5.6 copy-start.20
  11.7 5.9 copy-start.21
  12.4 18.4 %copy-start.15 = (f32[1024]{0:T(1024)}, f32[1024]{0:T(1024)S(1)}, u32[]{:S(2)}) copy-start(f32[1024]{0:T(1024)S(1)} %fusion.15) | copy-start | bytes 12292
  131.7 1.7 copy-start.2
  230.4 15.8 %copy-start.7 = (f32[1024,2304]{1,0:T(8,128)S(1)}, f32[1024,2304]{1,0:T(8,128)}, u32[]{:S(2)}) copy-start(f32[1024,2304]{1,0:T(8,128)} %fusion.34) | copy-start | bytes 28311556
  246.1 7.8 %copy-start.10 = (f32[1024,1152]{1,0:T(8,128)}, f32[1024,1152]{1,0:T(8,128)S(1)}, u32[]{:S(2)}) copy-start(f32[1024,1152]{1,0:T(8,128)S(1)} %get-tuple-element.32) | copy-start | bytes 14155780
  246.1 7.8 %copy-start.3 = (f32[1024,768]{1,0:T(8,128)S(1)}, f32[1024,768]{1,0:T(8,128)}, u32[]{:S(2)}) copy-start(f32[1024,768]{1,0:T(8,128)} %copy-done.2) | copy-start | bytes 9437188
  253.9 8.7 %copy-start.5 = (f32[1024,1152]{1,0:T(8,128)}, f32[1024,1152]{1,0:T(8,128)S(1)}, u32[]{:S(2)}) copy-start(f32[1024,1152]{1,0:T(8,128)S(1)} %get-tuple-element.34) | copy-start | bytes 14155780
  262.6 1.5 copy-start.8
  264.1 1.6 copy-start.4
  264.1 1.6 copy-start.13
  265.7 1.1 copy-start.12
  269.4 131.2 %reduce-scatter.11.cloned.1.call-start = ((), (), s32[]{:S(2)}) async-start(), calls=%async_computation.11 | async-start | bytes 1990656 | tf_op jit(solution)/shard_map/reduce_scatter | solution.py:209
  275.0 209.2 %reduce-scatter.9.cloned.1.call-start = ((), (), s32[]{:S(2)}) async-start(), calls=%async_computation.10 | async-start | bytes 3981312 | tf_op jit(solution)/shard_map/reduce_scatter | solution.py:209
  285.7 281.1 %reduce-scatter.5.cloned.1.call-start = ((), (), s32[]{:S(2)}) async-start(), calls=%async_computation.8 | async-start | bytes 3981312 | tf_op jit(solution)/shard_map/reduce_scatter | solution.py:209
  290.3 38.3 %copy-start.11 = (bf16[1024,768]{1,0:T(8,128)(2,1)S(1)}, bf16[1024,768]{1,0:T(8,128)(2,1)}, u32[]{:S(2)}) copy-start(bf16[1024,768]{1,0:T(8,128)(2,1)} %fusion.13.a_ref) | copy-start | bytes 4718596
  340.9 1.4 copy-start.1
  340.9 267.4 %all-reduce.12.cloned.1.call-start = ((), (), s32[]{:S(2)}) async-start(), calls=%async_computation.12 | async-start | bytes 2506752 | tf_op jit(solution)/shard_map/psum | solution.py:212
  342.3 7.2 %copy-start.16 = (f32[1024]{0:T(1024)S(1)}, f32[1024]{0:T(1024)}, u32[]{:S(2)}) copy-start(f32[1024]{0:T(1024)} %copy-done.15) | copy-start | bytes 12292
  349.5 1.6 copy-start.6
  349.5 3.3 copy-start.18
  349.5 26.2 %copy-start.9 = (bf16[1024,768]{1,0:T(8,128)(2,1)S(1)}, bf16[1024,768]{1,0:T(8,128)(2,1)}, u32[]{:S(2)}) copy-start(bf16[1024,768]{1,0:T(8,128)(2,1)} %param.17) | copy-start | bytes 4718596
  349.5 26.2 %copy-start.14 = (f32[1024]{0:T(1024)S(1)}, f32[1024]{0:T(1024)}, u32[]{:S(2)}) copy-start(f32[1024]{0:T(1024)} %copy-done.13) | copy-start | bytes 12292
Sparse Core Ops, SparseCore 0:
  10.2 64.2 all-gather.4
  76.6 39.6 all-gather.6
  118.5 63.8 all-gather.8
  184.5 45.8 all-gather.10
  269.5 62.2 reduce-scatter.6
  335.1 65.4 reduce-scatter.10
  404.7 79.4 reduce-scatter.8
  488.3 78.4 reduce-scatter.4
  569.7 38.6 all-reduce.11
